TPU v7x, 128 devices: a whole 4x4x4 slice. The times are simulated.
128 devices in a mesh: dp: 4 (over y), pipe: 4 (over z), expert: 8 (over x, core).
Axes of the slice: x: 4, y: 4, z: 4, core: 2. Of those that a mesh axis runs over, the one named last changes fastest.
Arguments:
- tokens: bfloat16 [4, 4096, 5120], P('pipe', ('dp', 'expert')), may hold values from -6 to 6
- cotangent: bfloat16 [4, 4096, 5120], P('pipe', ('dp', 'expert')), may hold values from -6 to 6
- gain: float32 [4, 5120], P('pipe'), may hold values from 0.1 to 1.9
- w_gate: bfloat16 [4, 8, 5120, 768], P('pipe', 'expert', 'dp'), may hold values from -0.078125 to 0.078125
- w_up: bfloat16 [4, 8, 5120, 768], P('pipe', 'expert', 'dp'), may hold values from -0.078125 to 0.078125
- w_down: bfloat16 [4, 8, 768, 5120], P('pipe', 'expert', None, 'dp'), may hold values from -0.21875 to 0.21875
- route: int32 [4, 4, 512, 1], P('pipe', None, ('dp', 'expert')), may hold values from 0 to 7; in each aligned block of 16 rows (0 to 15, 16 to 31, ..., all dimensions but the last counted through in order) at most 3 rows name the same one
Outputs:
- out_tokens: bfloat16 [4, 4096, 5120], P('pipe', ('dp', 'expert'))
- grad_tokens: bfloat16 [4, 4096, 5120], P('pipe', ('dp', 'expert'))
- grad_gain: float32 [4, 5120], P('pipe')
- grad_gate: bfloat16 [4, 8, 5120, 768], P('pipe', 'expert', 'dp')
- grad_up: bfloat16 [4, 8, 5120, 768], P('pipe', 'expert', 'dp')
- grad_down: bfloat16 [4, 8, 768, 5120], P('pipe', 'expert', None, 'dp')
Inputs may be any that keep to these rules, and one draw needn't show every extreme that they name: route[l, m, t, 0] is the expert of tile t at layer l for micro-batch m. Among the 16 tiles of one device for one layer and one micro-batch (aligned blocks), no expert is named more than 3 times; every expert is named somewhere.
All inputs are finite; a program needn't handle non-finite values.
Results may differ from a plain program's by a relative error of at most 0.034.
Values may be sent and summed in bfloat16 or wider, within the bound.
A program may use at most 128 MiB of HBM per device.

v0:
```python
import jax
import jax.numpy as jnp
from jax import lax
from jax.sharding import PartitionSpec as P

TILE = 8
PASSES = 2
epsilon = 1e-06


def shifted(block, axis, distance):
    devices = range(lax.axis_size(axis))
    route = [((i - distance) % len(devices), i) for i in devices]
    return lax.ppermute(block, axis, route)


def contract_last(former, latter):
    return lax.dot_general(
        former, latter, (((1,), (1,)), ((), ())), preferred_element_type=jnp.float32
    )


def contract_first(former, latter):
    return lax.dot_general(
        former, latter, (((0,), (0,)), ((), ())), preferred_element_type=jnp.float32
    )


def normalize(hidden, gain_row):
    widened = hidden.astype(jnp.float32)
    inverse = lax.rsqrt(jnp.mean(widened * widened, axis=-1, keepdims=True) + epsilon)
    scaled = widened * inverse
    return ((scaled * gain_row).astype(jnp.bfloat16), scaled, inverse)


def slot_matrix(route_now, expert_count, capacity):
    tile_count = route_now.shape[0]
    expert_ids = jnp.arange(expert_count, dtype=jnp.int32)
    member = (route_now[None, :] == expert_ids[:, None]).astype(jnp.int32)
    earlier = jnp.cumsum(member, axis=1) - member
    rank_ids = jnp.arange(capacity, dtype=jnp.int32)
    placed = member[:, None, :] * (earlier[:, None, :] == rank_ids[None, :, None]).astype(jnp.int32)
    return placed.reshape(expert_count * capacity, tile_count)


def into_slots(placed, rows, tile_rows, dp_count):
    width = rows.shape[-1]
    tile_blocks = rows.reshape(placed.shape[1], tile_rows, dp_count, width // dp_count)
    return jnp.einsum(
        "st,trqd->qsrd",
        placed.astype(jnp.bfloat16),
        tile_blocks,
        preferred_element_type=jnp.float32,
    ).astype(jnp.bfloat16)


def from_slots(placed, slot_rows):
    merged = jnp.einsum(
        "st,qsrd->trqd", placed.astype(jnp.bfloat16), slot_rows, preferred_element_type=jnp.float32
    ).astype(jnp.bfloat16)
    return merged.reshape(merged.shape[0] * merged.shape[1], -1)


def send_out(slot_rows):
    quarter = slot_rows.shape[-1]
    flat = slot_rows.reshape((-1,) + slot_rows.shape[2:])
    arrived = lax.all_to_all(flat, ("dp", "expert"), split_axis=0, concat_axis=0, tiled=True)
    return arrived.reshape(-1, quarter)


def send_back(part_rows, dp_count, tile_rows):
    quarter = part_rows.shape[-1]
    flat = part_rows.reshape(-1, tile_rows, quarter)
    returned = lax.all_to_all(flat, ("dp", "expert"), split_axis=0, concat_axis=0, tiled=True)
    return returned.reshape(dp_count, -1, tile_rows, quarter)


def widen_rounded(values):
    return lax.optimization_barrier(values.astype(jnp.bfloat16)).astype(jnp.float32)


def expert_forward(received, gate_weight, up_weight, down_weight):
    gate_terms = widen_rounded(jnp.dot(received, gate_weight, preferred_element_type=jnp.float32))
    up_terms = widen_rounded(jnp.dot(received, up_weight, preferred_element_type=jnp.float32))
    gate_pre, up_pre = (
        lax.psum(gate_terms.astype(jnp.bfloat16), "dp").astype(jnp.float32),
        lax.psum(up_terms.astype(jnp.bfloat16), "dp").astype(jnp.float32),
    )
    activated = (jax.nn.silu(gate_pre) * up_pre).astype(jnp.bfloat16)
    part_rows = jnp.dot(activated, down_weight, preferred_element_type=jnp.float32).astype(
        jnp.bfloat16
    )
    return (part_rows, (gate_pre, up_pre, activated))


def expert_backward(
    received, grad_recv, kept_state, gate_weight, up_weight, down_weight, grad_sums
):
    gate_pre, up_pre, activated = kept_state
    grad_terms = widen_rounded(contract_last(grad_recv, down_weight))
    grad_act = lax.psum(grad_terms.astype(jnp.bfloat16), "dp").astype(jnp.float32)
    sigmoid_gate = jax.nn.sigmoid(gate_pre)
    silu_gate = gate_pre * sigmoid_gate
    grad_gate_pre = (
        grad_act * up_pre * sigmoid_gate * (1.0 + gate_pre * (1.0 - sigmoid_gate))
    ).astype(jnp.bfloat16)
    grad_up_pre = (grad_act * silu_gate).astype(jnp.bfloat16)
    back_rows = (
        contract_last(grad_gate_pre, gate_weight) + contract_last(grad_up_pre, up_weight)
    ).astype(jnp.bfloat16)
    grad_gate = grad_sums[0] + contract_first(received, grad_gate_pre)
    grad_up = grad_sums[1] + contract_first(received, grad_up_pre)
    grad_down = grad_sums[2] + contract_first(activated, grad_recv)
    return (back_rows, (grad_gate, grad_up, grad_down))


def body(tokens, cotangent, gain, w_gate, w_up, w_down, route):
    pipe_count = lax.axis_size("pipe")
    dp_count = lax.axis_size("dp")
    expert_count = lax.axis_size("expert")
    section_index = lax.axis_index("pipe")
    gain_row = gain[0]
    gate_weight = w_gate[0, 0]
    up_weight = w_up[0, 0]
    down_weight = w_down[0, 0]
    route_table = route[0, :, :, 0]
    tile_count = route_table.shape[1]
    capacity = max(2, 3 * tile_count // (2 * expert_count))
    hidden = tokens[0]
    saved_ticks = []
    out_rows = hidden
    for pass_index in range(PASSES):
        micro_index = (section_index - pass_index + pipe_count) % pipe_count
        route_now = lax.dynamic_index_in_dim(route_table, micro_index, 0, keepdims=False)
        placed = slot_matrix(route_now, expert_count, capacity)
        normed, scaled, inverse = normalize(hidden, gain_row)
        received = send_out(into_slots(placed, normed, TILE, dp_count))
        part_rows, kept_state = expert_forward(received, gate_weight, up_weight, down_weight)
        ffn_rows = from_slots(placed, send_back(part_rows, dp_count, TILE))
        new_hidden = (hidden.astype(jnp.float32) + ffn_rows.astype(jnp.float32)).astype(
            jnp.bfloat16
        )
        saved_ticks.append((placed, scaled, inverse, received, kept_state))
        if pass_index + 1 < PASSES:
            hidden = shifted(new_hidden, "pipe", 1)
        else:
            out_rows = new_hidden
    grad_rows = cotangent[0]
    grad_sums = (
        jnp.zeros(gate_weight.shape, jnp.float32),
        jnp.zeros(up_weight.shape, jnp.float32),
        jnp.zeros(down_weight.shape, jnp.float32),
    )
    gain_sum = jnp.zeros(gain_row.shape, jnp.float32)
    entry_grad = grad_rows
    for pass_index in reversed(range(PASSES)):
        placed, scaled, inverse, received, kept_state = saved_ticks[pass_index]
        grad_recv = send_out(into_slots(placed, grad_rows, TILE, dp_count))
        back_rows, grad_sums = expert_backward(
            received, grad_recv, kept_state, gate_weight, up_weight, down_weight, grad_sums
        )
        grad_normed = from_slots(placed, send_back(back_rows, dp_count, TILE)).astype(jnp.float32)
        gain_sum = gain_sum + jnp.sum(grad_normed * scaled, axis=0)
        grad_scaled = grad_normed * gain_row
        grad_wide = inverse * (
            grad_scaled - scaled * jnp.mean(grad_scaled * scaled, axis=-1, keepdims=True)
        )
        grad_in = (grad_rows.astype(jnp.float32) + grad_wide).astype(jnp.bfloat16)
        if pass_index > 0:
            grad_rows = shifted(grad_in, "pipe", -1)
        else:
            entry_grad = grad_in
    gain_total = lax.psum(gain_sum, ("dp", "expert"))
    return (
        out_rows[None],
        entry_grad[None],
        gain_total[None],
        grad_sums[0].astype(jnp.bfloat16)[None, None],
        grad_sums[1].astype(jnp.bfloat16)[None, None],
        grad_sums[2].astype(jnp.bfloat16)[None, None],
    )


def solution(mesh):
    placed = (
        P("pipe", ("dp", "expert"), None),
        P("pipe", ("dp", "expert"), None),
        P("pipe", None),
        P("pipe", "expert", "dp", None),
        P("pipe", "expert", "dp", None),
        P("pipe", "expert", None, "dp"),
        P("pipe", None, ("dp", "expert"), None),
    )
    return jax.shard_map(
        body,
        mesh=mesh,
        in_specs=placed,
        out_specs=(
            P("pipe", ("dp", "expert"), None),
            P("pipe", ("dp", "expert"), None),
            P("pipe", None),
            P("pipe", "expert", "dp", None),
            P("pipe", "expert", "dp", None),
            P("pipe", "expert", None, "dp"),
        ),
        check_vma=False,
    )
```

profile of v0, /device:TPU:0, one launch (start us, length us, event | category | flops | bytes accessed | tf_op | source)
XLA Modules:
  0.0 713.0 jit_solution(6603323839218652019)
XLA Ops:
  13.2 34.5 %all_to_all.40 = bf16[96,8,1280]{2,1,0:T(8,128)(2,1)S(1)} all-to-all(bf16[96,8,1280]{2,1,0:T(8,128)(2,1)S(1)} %copy.49), channel_id=1, replica_groups=mesh['dp'=4,'pipe'=4,'expert'=8] {'dp','expert'}, dimensions={0} | all-to-all | bytes 3932160 | tf_op jit(solution)/shard_map/all_to_all | solution.py:67
  53.2 62.0 %all-reduce.10.cloned.1.call-done = (bf16[768,768]{1,0:T(8,128)(2,1)}, bf16[768,768]{1,0:T(8,128)(2,1)}) async-done(((bf16[768,768]{1,0:T(8,128)(2,1)}, bf16[768,768]{1,0:T(8,128)(2,1)}), (bf16[768,768]{1,0:T(8,128)(2,1)}, bf16[768,768]{1,0:T(8,128)(2,1)})) %all-reduce.10.cloned.1.call-update) | async-done | bytes 2359312 | tf_op jit(solution)/shard_map/psum | solution.py:87
  118.9 32.6 %all_to_all.41 = bf16[96,8,1280]{2,1,0:T(8,128)(2,1)S(1)} all-to-all(bf16[96,8,1280]{2,1,0:T(8,128)(2,1)S(1)} %fusion.12), channel_id=1, replica_groups=mesh['dp'=4,'pipe'=4,'expert'=8] {'dp','expert'}, dimensions={0} | all-to-all | bytes 3932160 | tf_op jit(solution)/shard_map/all_to_all | solution.py:74
  163.1 4.9 all-to-all-start.4
  167.9 20.4 %collective-permute-done = bf16[128,5120]{1,0:T(8,128)(2,1)} collective-permute-done((bf16[128,5120]{1,0:T(8,128)(2,1)}, bf16[128,5120]{1,0:T(8,128)(2,1)}, u32[]{:S(2)}, u32[]{:S(2)}) %collective-permute-start) | collective-permute-done | bytes 1310752 | tf_op jit(solution)/shard_map/ppermute | solution.py:14
  196.4 4.7 all-to-all-start.2
  201.2 4.3 fusion.114
  205.4 24.1 %all-to-all-done.2 = bf16[96,8,1280]{2,1,0:T(8,128)(2,1)} async-done(((bf16[96,8,1280]{2,1,0:T(8,128)(2,1)}), bf16[96,8,1280]{2,1,0:T(8,128)(2,1)}, u32[]{:S(2)}, u32[]{:S(2)}) %all-to-all-start.2) | async-done | bytes 1966112 | tf_op jit(solution)/shard_map/all_to_all | solution.py:67
  229.5 5.0 fusion.104
  234.5 4.3 fusion.109
  238.8 79.5 %all-reduce.8.cloned.1.call-done = (bf16[768,768]{1,0:T(8,128)(2,1)}, bf16[768,768]{1,0:T(8,128)(2,1)}, bf16[768,768]{1,0:T(8,128)(2,1)}) async-done(((bf16[768,768]{1,0:T(8,128)(2,1)}, bf16[768,768]{1,0:T(8,128)(2,1)}, bf16[768,768]{1,0:T(8,128)(2,1)}), (bf16[768,768]{1,0:T(8,128)(2,1)}, bf16[768,768]{1,0:T(8,128)(2,1)}, bf16[768,768]{1,0:T(8,128)(2,1)})) %all-reduce.8.cloned.1.call-update) | async-done | bytes 3538960 | tf_op jit(solution)/shard_map/psum | solution.py:87
  318.3 5.0 fusion.13
  323.4 5.9 all-to-all-start.3
  329.3 5.3 fusion.81
  338.1 19.6 %all-to-all-done.3 = bf16[96,8,1280]{2,1,0:T(8,128)(2,1)} async-done(((bf16[96,8,1280]{2,1,0:T(8,128)(2,1)}), bf16[96,8,1280]{2,1,0:T(8,128)(2,1)}, u32[]{:S(2)}, u32[]{:S(2)}) %all-to-all-start.3) | async-done | bytes 1966112 | tf_op jit(solution)/shard_map/all_to_all | solution.py:74
  357.7 4.7 all-to-all-start.5
  368.2 22.7 %all-to-all-done.5 = bf16[96,8,1280]{2,1,0:T(8,128)(2,1)} async-done(((bf16[96,8,1280]{2,1,0:T(8,128)(2,1)}), bf16[96,8,1280]{2,1,0:T(8,128)(2,1)}, u32[]{:S(2)}, u32[]{:S(2)}) %all-to-all-start.5) | async-done | bytes 1966112 | tf_op jit(solution)/shard_map/all_to_all | solution.py:74
  404.1 26.3 %collective-permute-done.1 = bf16[128,5120]{1,0:T(8,128)(2,1)} collective-permute-done((bf16[128,5120]{1,0:T(8,128)(2,1)S(1)}, bf16[128,5120]{1,0:T(8,128)(2,1)}, u32[]{:S(2)}, u32[]{:S(2)}) %collective-permute-start.1) | collective-permute-done | bytes 1310752 | tf_op jit(solution)/shard_map/ppermute | solution.py:14
  438.7 5.3 all-to-all-start.6
  448.3 5.9 fusion.62
  454.2 18.3 %all-to-all-done.6 = bf16[96,8,1280]{2,1,0:T(8,128)(2,1)} async-done(((bf16[96,8,1280]{2,1,0:T(8,128)(2,1)}), bf16[96,8,1280]{2,1,0:T(8,128)(2,1)}, u32[]{:S(2)}, u32[]{:S(2)}) %all-to-all-start.6) | async-done | bytes 1966112 | tf_op jit(solution)/shard_map/all_to_all | solution.py:67
  472.5 4.3 fusion.119
  476.8 6.1 fusion.58
  482.9 5.5 fusion.64
  488.4 33.1 %all-reduce.6.cloned.1.call-done = bf16[768,768]{1,0:T(8,128)(2,1)} async-done(((bf16[768,768]{1,0:T(8,128)(2,1)}), bf16[768,768]{1,0:T(8,128)(2,1)}) %all-reduce.6.cloned.1.call-update) | async-done | bytes 1179664 | tf_op jit(solution)/shard_map/psum | solution.py:101
  521.5 5.3 fusion.79
  530.4 6.8 all-to-all-start.7
  537.3 6.7 fusion.18
  550.5 15.1 %all-to-all-done.7 = bf16[96,8,1280]{2,1,0:T(8,128)(2,1)} async-done(((bf16[96,8,1280]{2,1,0:T(8,128)(2,1)}), bf16[96,8,1280]{2,1,0:T(8,128)(2,1)}, u32[]{:S(2)}, u32[]{:S(2)}) %all-to-all-start.7) | async-done | bytes 1966112 | tf_op jit(solution)/shard_map/all_to_all | solution.py:74
  565.6 5.9 multiply_reduce_fusion
  571.5 125.2 %psum.55 = f32[1,5120]{1,0:T(1,128)} all-reduce(f32[1,5120]{1,0:T(1,128)S(1)} %bitcast.217), channel_id=1, replica_groups=mesh['dp'=4,'pipe'=4,'expert'=8] {'dp','expert'}, use_global_device_ids=true, to_apply=%region_14.15 | all-reduce | flops 5120 | bytes 40960 | tf_op jit(solution)/shard_map/psum | solution.py:173
  702.3 4.0 fusion.124
  (115 shorter events, 85.3 us)
Async XLA Ops:
  7.2 108.0 %copy-start = (bf16[1,1,768,1280]{3,2,1,0:T(8,128)(2,1)S(1)}, bf16[1,1,768,1280]{3,2,1,0:T(8,128)(2,1)}, u32[]{:S(2)}) copy-start(bf16[1,1,768,1280]{3,2,1,0:T(8,128)(2,1)} %param.12) | copy-start | bytes 5898244
  7.2 2.8 copy-start.1
  7.2 108.0 %all-reduce.10.cloned.1.call-start = ((), (), s32[]{:S(2)}) async-start(), calls=%async_computation.10 | async-start | bytes 4718592 | tf_op jit(solution)/shard_map/psum | solution.py:87
  13.2 34.5 %copy-start.7 = (bf16[1,1,1280,768]{3,2,1,0:T(8,128)(2,1)S(1)}, bf16[1,1,1280,768]{3,2,1,0:T(8,128)(2,1)}, u32[]{:S(2)}) copy-start(bf16[1,1,1280,768]{3,2,1,0:T(8,128)(2,1)} %param.10) | copy-start | bytes 5898244
  47.7 2.7 copy-start.8
  155.6 32.8 %collective-permute-start = (bf16[128,5120]{1,0:T(8,128)(2,1)}, bf16[128,5120]{1,0:T(8,128)(2,1)}, u32[]{:S(2)}, u32[]{:S(2)}) collective-permute-start(bf16[128,5120]{1,0:T(8,128)(2,1)} %fusion.29), channel_id=1, source_target_pairs={{24,0},{0,8},{8,16},{16,24},{25,1},{1,9},{9,17},{17,25},{26,2},{2,... | collective-permute-start | bytes 3932168 | tf_op jit(solution)/shard_map/ppermute | solution.py:14
  163.1 27.0 %copy-start.6 = (f32[1,5120]{1,0:T(1,128)S(1)}, f32[1,5120]{1,0:T(1,128)}, u32[]{:S(2)}) copy-start(f32[1,5120]{1,0:T(1,128)} %param.9) | copy-start | bytes 61444
  163.1 33.3 %all-to-all-start.4 = ((bf16[96,8,1280]{2,1,0:T(8,128)(2,1)}), bf16[96,8,1280]{2,1,0:T(8,128)(2,1)}, u32[]{:S(2)}, u32[]{:S(2)}) async-start(bf16[96,8,1280]{2,1,0:T(8,128)(2,1)} %copy.61), calls=%async_computation.4 | async-start | bytes 3932160 | tf_op jit(solution)/shard_map/all_to_all | solution.py:67
  196.4 33.2 %all-to-all-start.2 = ((bf16[96,8,1280]{2,1,0:T(8,128)(2,1)}), bf16[96,8,1280]{2,1,0:T(8,128)(2,1)}, u32[]{:S(2)}, u32[]{:S(2)}) async-start(bf16[96,8,1280]{2,1,0:T(8,128)(2,1)} %copy.55), calls=%async_computation.2 | async-start | bytes 3932160 | tf_op jit(solution)/shard_map/all_to_all | solution.py:67
  201.1 117.2 %all-reduce.8.cloned.1.call-start = ((), (), s32[]{:S(2)}) async-start(), calls=%async_computation.9 | async-start | bytes 7077888 | tf_op jit(solution)/shard_map/psum | solution.py:87
  229.5 5.0 copy-start.9
  323.4 34.3 %all-to-all-start.3 = ((bf16[96,8,1280]{2,1,0:T(8,128)(2,1)}), bf16[96,8,1280]{2,1,0:T(8,128)(2,1)}, u32[]{:S(2)}, u32[]{:S(2)}) async-start(bf16[96,8,1280]{2,1,0:T(8,128)(2,1)} %fusion.13), calls=%async_computation.3 | async-start | bytes 3932160 | tf_op jit(solution)/shard_map/all_to_all | solution.py:74
  329.3 5.3 copy-start.10
  329.3 5.3 copy-start.16
  329.3 5.3 copy-start.18
  357.7 33.2 %all-to-all-start.5 = ((bf16[96,8,1280]{2,1,0:T(8,128)(2,1)}), bf16[96,8,1280]{2,1,0:T(8,128)(2,1)}, u32[]{:S(2)}, u32[]{:S(2)}) async-start(bf16[96,8,1280]{2,1,0:T(8,128)(2,1)} %fusion.14), calls=%async_computation.5 | async-start | bytes 3932160 | tf_op jit(solution)/shard_map/all_to_all | solution.py:74
  401.2 29.2 %collective-permute-start.1 = (bf16[128,5120]{1,0:T(8,128)(2,1)S(1)}, bf16[128,5120]{1,0:T(8,128)(2,1)}, u32[]{:S(2)}, u32[]{:S(2)}) collective-permute-start(bf16[128,5120]{1,0:T(8,128)(2,1)S(1)} %get-tuple-element.15), channel_id=1, source_target_pairs={{8,0},{16,8},{24,16},{0,24},{9,1},{17,9},{25,17},{1,25},{10,2},{18... | collective-permute-start | bytes 3932168 | tf_op jit(solution)/shard_map/ppermute | solution.py:14
  438.7 33.7 %all-to-all-start.6 = ((bf16[96,8,1280]{2,1,0:T(8,128)(2,1)}), bf16[96,8,1280]{2,1,0:T(8,128)(2,1)}, u32[]{:S(2)}, u32[]{:S(2)}) async-start(bf16[96,8,1280]{2,1,0:T(8,128)(2,1)} %copy.67), calls=%async_computation.6 | async-start | bytes 3932160 | tf_op jit(solution)/shard_map/all_to_all | solution.py:67
  444.0 77.5 %all-reduce.6.cloned.1.call-start = ((), (), s32[]{:S(2)}) async-start(), calls=%async_computation.8 | async-start | bytes 2359296 | tf_op jit(solution)/shard_map/psum | solution.py:101
  476.8 6.2 copy-start.15
  476.8 6.1 copy-start.17
  476.8 6.1 copy-start.19
  521.5 5.3 copy-start.11
  521.5 5.3 copy-start.13
  521.5 5.3 copy-start.20
  530.4 35.3 %all-to-all-start.7 = ((bf16[96,8,1280]{2,1,0:T(8,128)(2,1)}), bf16[96,8,1280]{2,1,0:T(8,128)(2,1)}, u32[]{:S(2)}, u32[]{:S(2)}) async-start(bf16[96,8,1280]{2,1,0:T(8,128)(2,1)} %fusion.15), calls=%async_computation.7 | async-start | bytes 3932160 | tf_op jit(solution)/shard_map/all_to_all | solution.py:74
  537.2 6.8 copy-start.5
  537.2 6.8 copy-start.14
  537.2 6.8 copy-start.21
  537.2 6.8 copy-start.22
  544.0 3.2 copy-start.12
  544.0 3.2 copy-start.23
  (3 other events, 7.7 us)
Sparse Core Ops, SparseCore 0:
  53.3 61.8 all-reduce.9
  238.9 79.3 all-reduce.7
  476.9 44.5 all-reduce.5
where the time goes:
time: 723 us; the launch traced here: 713 us
  waiting for transfers between devices  322 us (45%)
  blocking collectives  192 us (27%)
  matrix products  98 us (14%)
  starting transfers between devices  37.9 us (5%)
  local copies, waits for them, and re-layouts  29.4 us (4%)
  other arithmetic  18.6 us (3%)
  between operations  14.4 us (2%)
    psum x2, waiting for transfers between devices, expert_forward(): lax.psum(up_terms.astype(jnp.bfloat16), 'dp').astype(jnp.float32)  142 us
    psum x1, blocking collectives, body(): gain_total = lax.psum(gain_sum, ('dp', 'expert'))  125 us
    all_to_all x3, waiting for transfers between devices, send_back(): lax.all_to_all(flat, ('dp', 'expert'), split_axis=0, concat_axis=0, tiled...  57.4 us
    ppermute x2, waiting for transfers between devices, shifted(): return lax.ppermute(block, axis, route)  46.7 us
    all_to_all x3, waiting for transfers between devices, send_out(): lax.all_to_all(flat, ('dp', 'expert'), split_axis=0, concat_axis=0, tiled...  43.6 us
    all_to_all x1, blocking collectives, send_out(): lax.all_to_all(flat, ('dp', 'expert'), split_axis=0, concat_axis=0, tiled...  34.5 us
    psum x1, waiting for transfers between devices, expert_backward(): lax.psum(grad_terms.astype(jnp.bfloat16), 'dp').astype(jnp.float32)  33.1 us
    all_to_all x1, blocking collectives, send_back(): lax.all_to_all(flat, ('dp', 'expert'), split_axis=0, concat_axis=0, tiled...  32.6 us
  transfers between devices with their start and end apart: 11, of which 11 were waited for; matrix products, arithmetic and copies ran while one was open for 9% of the time, Pallas kernels for 0%

commit v1 on v0

--- a/solution.py
+++ b/solution.py
@@ -170,7 +170,7 @@
             grad_rows = shifted(grad_in, "pipe", -1)
         else:
             entry_grad = grad_in
-    gain_total = lax.psum(gain_sum, ("dp", "expert"))
+    gain_total = lax.psum(lax.psum(gain_sum, "expert"), "dp")
     return (
         out_rows[None],
         entry_grad[None],

time: 723 us -> 638 us (0.88)
  blocking collectives: 192 us -> 108 us
    psum x1 -> x2, blocking collectives: 125 us -> 40.6 us  [body(): gain_total = lax.psum(lax.psum(gain_sum, 'expert'), 'dp')]
  transfers between devices with their start and end apart: 11 -> 11, of which waited for: 11 -> 11; matrix products, arithmetic and copies ran while one was open for 9% -> 10% of each run, Pallas kernels for 0% -> 0%
where the time goes in v1:
time: 638 us; the launch traced here: 629 us
  waiting for transfers between devices  322 us (50%)
  blocking collectives  108 us (17%)
  matrix products  98 us (15%)
  starting transfers between devices  38 us (6%)
  local copies, waits for them, and re-layouts  29.4 us (5%)
  other arithmetic  18.6 us (3%)
  between operations  14.5 us (2%)
    psum x2, waiting for transfers between devices, expert_forward(): lax.psum(up_terms.astype(jnp.bfloat16), 'dp').astype(jnp.float32)  142 us
    all_to_all x3, waiting for transfers between devices, send_back(): lax.all_to_all(flat, ('dp', 'expert'), split_axis=0, concat_axis=0, tiled...  57.5 us
    ppermute x2, waiting for transfers between devices, shifted(): return lax.ppermute(block, axis, route)  46.7 us
    all_to_all x3, waiting for transfers between devices, send_out(): lax.all_to_all(flat, ('dp', 'expert'), split_axis=0, concat_axis=0, tiled...  43.6 us
    psum x2, blocking collectives, body(): gain_total = lax.psum(lax.psum(gain_sum, 'expert'), 'dp')  40.6 us
    all_to_all x1, blocking collectives, send_out(): lax.all_to_all(flat, ('dp', 'expert'), split_axis=0, concat_axis=0, tiled...  34.5 us
    psum x1, waiting for transfers between devices, expert_backward(): lax.psum(grad_terms.astype(jnp.bfloat16), 'dp').astype(jnp.float32)  33.1 us
    all_to_all x1, blocking collectives, send_back(): lax.all_to_all(flat, ('dp', 'expert'), split_axis=0, concat_axis=0, tiled...  32.6 us
  transfers between devices with their start and end apart: 11, of which 11 were waited for; matrix products, arithmetic and copies ran while one was open for 10% of the time, Pallas kernels for 0%

profile of v1, /device:TPU:0, one launch (start us, length us, event | category | flops | bytes accessed | tf_op | source)
XLA Modules:
  0.0 628.5 jit_solution(6849159920684291103)
XLA Ops:
  13.2 34.5 %all_to_all.40 = bf16[96,8,1280]{2,1,0:T(8,128)(2,1)S(1)} all-to-all(bf16[96,8,1280]{2,1,0:T(8,128)(2,1)S(1)} %copy.49), channel_id=1, replica_groups=mesh['dp'=4,'pipe'=4,'expert'=8] {'dp','expert'}, dimensions={0} | all-to-all | bytes 3932160 | tf_op jit(solution)/shard_map/all_to_all | solution.py:67
  53.2 62.0 %all-reduce.10.cloned.1.call-done = (bf16[768,768]{1,0:T(8,128)(2,1)}, bf16[768,768]{1,0:T(8,128)(2,1)}) async-done(((bf16[768,768]{1,0:T(8,128)(2,1)}, bf16[768,768]{1,0:T(8,128)(2,1)}), (bf16[768,768]{1,0:T(8,128)(2,1)}, bf16[768,768]{1,0:T(8,128)(2,1)})) %all-reduce.10.cloned.1.call-update) | async-done | bytes 2359312 | tf_op jit(solution)/shard_map/psum | solution.py:87
  118.9 32.6 %all_to_all.41 = bf16[96,8,1280]{2,1,0:T(8,128)(2,1)S(1)} all-to-all(bf16[96,8,1280]{2,1,0:T(8,128)(2,1)S(1)} %fusion.12), channel_id=1, replica_groups=mesh['dp'=4,'pipe'=4,'expert'=8] {'dp','expert'}, dimensions={0} | all-to-all | bytes 3932160 | tf_op jit(solution)/shard_map/all_to_all | solution.py:74
  163.1 4.9 all-to-all-start.4
  168.0 20.4 %collective-permute-done = bf16[128,5120]{1,0:T(8,128)(2,1)} collective-permute-done((bf16[128,5120]{1,0:T(8,128)(2,1)}, bf16[128,5120]{1,0:T(8,128)(2,1)}, u32[]{:S(2)}, u32[]{:S(2)}) %collective-permute-start) | collective-permute-done | bytes 1310752 | tf_op jit(solution)/shard_map/ppermute | solution.py:14
  196.4 4.7 all-to-all-start.2
  201.2 4.3 fusion.114
  205.5 24.1 %all-to-all-done.2 = bf16[96,8,1280]{2,1,0:T(8,128)(2,1)} async-done(((bf16[96,8,1280]{2,1,0:T(8,128)(2,1)}), bf16[96,8,1280]{2,1,0:T(8,128)(2,1)}, u32[]{:S(2)}, u32[]{:S(2)}) %all-to-all-start.2) | async-done | bytes 1966112 | tf_op jit(solution)/shard_map/all_to_all | solution.py:67
  229.6 5.0 fusion.104
  234.6 4.3 fusion.109
  238.9 79.5 %all-reduce.8.cloned.1.call-done = (bf16[768,768]{1,0:T(8,128)(2,1)}, bf16[768,768]{1,0:T(8,128)(2,1)}, bf16[768,768]{1,0:T(8,128)(2,1)}) async-done(((bf16[768,768]{1,0:T(8,128)(2,1)}, bf16[768,768]{1,0:T(8,128)(2,1)}, bf16[768,768]{1,0:T(8,128)(2,1)}), (bf16[768,768]{1,0:T(8,128)(2,1)}, bf16[768,768]{1,0:T(8,128)(2,1)}, bf16[768,768]{1,0:T(8,128)(2,1)})) %all-reduce.8.cloned.1.call-update) | async-done | bytes 3538960 | tf_op jit(solution)/shard_map/psum | solution.py:87
  318.4 5.0 fusion.13
  323.4 5.9 all-to-all-start.3
  329.4 5.3 fusion.81
  338.2 19.6 %all-to-all-done.3 = bf16[96,8,1280]{2,1,0:T(8,128)(2,1)} async-done(((bf16[96,8,1280]{2,1,0:T(8,128)(2,1)}), bf16[96,8,1280]{2,1,0:T(8,128)(2,1)}, u32[]{:S(2)}, u32[]{:S(2)}) %all-to-all-start.3) | async-done | bytes 1966112 | tf_op jit(solution)/shard_map/all_to_all | solution.py:74
  357.8 4.8 all-to-all-start.5
  368.3 22.7 %all-to-all-done.5 = bf16[96,8,1280]{2,1,0:T(8,128)(2,1)} async-done(((bf16[96,8,1280]{2,1,0:T(8,128)(2,1)}), bf16[96,8,1280]{2,1,0:T(8,128)(2,1)}, u32[]{:S(2)}, u32[]{:S(2)}) %all-to-all-start.5) | async-done | bytes 1966112 | tf_op jit(solution)/shard_map/all_to_all | solution.py:74
  404.2 26.3 %collective-permute-done.1 = bf16[128,5120]{1,0:T(8,128)(2,1)} collective-permute-done((bf16[128,5120]{1,0:T(8,128)(2,1)S(1)}, bf16[128,5120]{1,0:T(8,128)(2,1)}, u32[]{:S(2)}, u32[]{:S(2)}) %collective-permute-start.1) | collective-permute-done | bytes 1310752 | tf_op jit(solution)/shard_map/ppermute | solution.py:14
  438.8 5.3 all-to-all-start.6
  448.4 5.9 fusion.62
  454.3 18.3 %all-to-all-done.6 = bf16[96,8,1280]{2,1,0:T(8,128)(2,1)} async-done(((bf16[96,8,1280]{2,1,0:T(8,128)(2,1)}), bf16[96,8,1280]{2,1,0:T(8,128)(2,1)}, u32[]{:S(2)}, u32[]{:S(2)}) %all-to-all-start.6) | async-done | bytes 1966112 | tf_op jit(solution)/shard_map/all_to_all | solution.py:67
  472.6 4.3 fusion.119
  476.9 6.1 fusion.58
  483.0 5.5 fusion.64
  488.5 33.1 %all-reduce.6.cloned.1.call-done = bf16[768,768]{1,0:T(8,128)(2,1)} async-done(((bf16[768,768]{1,0:T(8,128)(2,1)}), bf16[768,768]{1,0:T(8,128)(2,1)}) %all-reduce.6.cloned.1.call-update) | async-done | bytes 1179664 | tf_op jit(solution)/shard_map/psum | solution.py:101
  521.6 5.3 fusion.79
  530.5 6.8 %all-to-all-start.7 = ((bf16[96,8,1280]{2,1,0:T(8,128)(2,1)}), bf16[96,8,1280]{2,1,0:T(8,128)(2,1)}, u32[]{:S(2)}, u32[]{:S(2)}) async-start(bf16[96,8,1280]{2,1,0:T(8,128)(2,1)} %fusion.15), calls=%async_computation.7 | async-start | bytes 3932160 | tf_op jit(solution)/shard_map/all_to_all | solution.py:74
  537.4 6.7 %fusion.18 = bf16[1,1,768,1280]{3,2,1,0:T(8,128)(2,1)} fusion(f32[768,1280]{1,0:T(8,128)} %fusion.58, bf16[96,8,1280]{2,1,0:T(8,128)(2,1)} %all-to-all-done.6, bf16[768,768]{1,0:T(8,128)(2,1)} %get-tuple-element.13, bf16[768,768]{1,0:T(8,128)(2,1)} %get-tuple-element.14), kind=kOutput, calls=%fused_computation.42 | convolution fusion | flops 1516634112 | bytes 10223616 | tf_op jit(solution)/shard_map/dot_general | solution.py:24
  550.6 15.2 %all-to-all-done.7 = bf16[96,8,1280]{2,1,0:T(8,128)(2,1)} async-done(((bf16[96,8,1280]{2,1,0:T(8,128)(2,1)}), bf16[96,8,1280]{2,1,0:T(8,128)(2,1)}, u32[]{:S(2)}, u32[]{:S(2)}) %all-to-all-start.7) | async-done | bytes 1966112 | tf_op jit(solution)/shard_map/all_to_all | solution.py:74
  565.7 5.9 multiply_reduce_fusion
  571.6 23.8 %psum.62 = f32[5120]{0:T(1024)S(1)} all-reduce(f32[5120]{0:T(1024)S(1)} %add.121), channel_id=1, replica_groups=mesh['dp'=4,'pipe'=4,'expert'=8] {'expert'}, use_global_device_ids=true, to_apply=%region_14.15 | all-reduce | flops 5120 | bytes 40960 | tf_op jit(solution)/shard_map/psum | solution.py:173
  595.4 16.8 %psum.63 = f32[1,5120]{1,0:T(1,128)} all-reduce(f32[1,5120]{1,0:T(1,128)S(1)} %bitcast.217), channel_id=1, replica_groups=mesh['dp'=4,'pipe'=4,'expert'=8] {'dp'}, use_global_device_ids=true, to_apply=%region_15.16 | all-reduce | flops 5120 | bytes 40960 | tf_op jit(solution)/shard_map/psum | solution.py:173
  (116 shorter events, 89.3 us)
Async XLA Ops:
  7.2 108.0 %copy-start = (bf16[1,1,768,1280]{3,2,1,0:T(8,128)(2,1)S(1)}, bf16[1,1,768,1280]{3,2,1,0:T(8,128)(2,1)}, u32[]{:S(2)}) copy-start(bf16[1,1,768,1280]{3,2,1,0:T(8,128)(2,1)} %param.12) | copy-start | bytes 5898244
  7.2 2.8 copy-start.1
  7.2 108.0 %all-reduce.10.cloned.1.call-start = ((), (), s32[]{:S(2)}) async-start(), calls=%async_computation.10 | async-start | bytes 4718592 | tf_op jit(solution)/shard_map/psum | solution.py:87
  13.2 34.5 %copy-start.7 = (bf16[1,1,1280,768]{3,2,1,0:T(8,128)(2,1)S(1)}, bf16[1,1,1280,768]{3,2,1,0:T(8,128)(2,1)}, u32[]{:S(2)}) copy-start(bf16[1,1,1280,768]{3,2,1,0:T(8,128)(2,1)} %param.10) | copy-start | bytes 5898244
  47.7 2.7 copy-start.8
  155.6 32.8 %collective-permute-start = (bf16[128,5120]{1,0:T(8,128)(2,1)}, bf16[128,5120]{1,0:T(8,128)(2,1)}, u32[]{:S(2)}, u32[]{:S(2)}) collective-permute-start(bf16[128,5120]{1,0:T(8,128)(2,1)} %fusion.29), channel_id=1, source_target_pairs={{24,0},{0,8},{8,16},{16,24},{25,1},{1,9},{9,17},{17,25},{26,2},{2,... | collective-permute-start | bytes 3932168 | tf_op jit(solution)/shard_map/ppermute | solution.py:14
  163.1 26.9 %copy-start.6 = (f32[1,5120]{1,0:T(1,128)S(1)}, f32[1,5120]{1,0:T(1,128)}, u32[]{:S(2)}) copy-start(f32[1,5120]{1,0:T(1,128)} %param.9) | copy-start | bytes 61444
  163.1 33.3 %all-to-all-start.4 = ((bf16[96,8,1280]{2,1,0:T(8,128)(2,1)}), bf16[96,8,1280]{2,1,0:T(8,128)(2,1)}, u32[]{:S(2)}, u32[]{:S(2)}) async-start(bf16[96,8,1280]{2,1,0:T(8,128)(2,1)} %copy.61), calls=%async_computation.4 | async-start | bytes 3932160 | tf_op jit(solution)/shard_map/all_to_all | solution.py:67
  196.4 33.2 %all-to-all-start.2 = ((bf16[96,8,1280]{2,1,0:T(8,128)(2,1)}), bf16[96,8,1280]{2,1,0:T(8,128)(2,1)}, u32[]{:S(2)}, u32[]{:S(2)}) async-start(bf16[96,8,1280]{2,1,0:T(8,128)(2,1)} %copy.55), calls=%async_computation.2 | async-start | bytes 3932160 | tf_op jit(solution)/shard_map/all_to_all | solution.py:67
  201.2 117.2 %all-reduce.8.cloned.1.call-start = ((), (), s32[]{:S(2)}) async-start(), calls=%async_computation.9 | async-start | bytes 7077888 | tf_op jit(solution)/shard_map/psum | solution.py:87
  229.6 5.0 copy-start.9
  323.4 34.3 %all-to-all-start.3 = ((bf16[96,8,1280]{2,1,0:T(8,128)(2,1)}), bf16[96,8,1280]{2,1,0:T(8,128)(2,1)}, u32[]{:S(2)}, u32[]{:S(2)}) async-start(bf16[96,8,1280]{2,1,0:T(8,128)(2,1)} %fusion.13), calls=%async_computation.3 | async-start | bytes 3932160 | tf_op jit(solution)/shard_map/all_to_all | solution.py:74
  329.4 5.3 copy-start.10
  329.4 5.3 copy-start.16
  329.4 5.3 copy-start.18
  357.8 33.2 %all-to-all-start.5 = ((bf16[96,8,1280]{2,1,0:T(8,128)(2,1)}), bf16[96,8,1280]{2,1,0:T(8,128)(2,1)}, u32[]{:S(2)}, u32[]{:S(2)}) async-start(bf16[96,8,1280]{2,1,0:T(8,128)(2,1)} %fusion.14), calls=%async_computation.5 | async-start | bytes 3932160 | tf_op jit(solution)/shard_map/all_to_all | solution.py:74
  401.3 29.2 %collective-permute-start.1 = (bf16[128,5120]{1,0:T(8,128)(2,1)S(1)}, bf16[128,5120]{1,0:T(8,128)(2,1)}, u32[]{:S(2)}, u32[]{:S(2)}) collective-permute-start(bf16[128,5120]{1,0:T(8,128)(2,1)S(1)} %get-tuple-element.15), channel_id=1, source_target_pairs={{8,0},{16,8},{24,16},{0,24},{9,1},{17,9},{25,17},{1,25},{10,2},{18... | collective-permute-start | bytes 3932168 | tf_op jit(solution)/shard_map/ppermute | solution.py:14
  438.8 33.7 %all-to-all-start.6 = ((bf16[96,8,1280]{2,1,0:T(8,128)(2,1)}), bf16[96,8,1280]{2,1,0:T(8,128)(2,1)}, u32[]{:S(2)}, u32[]{:S(2)}) async-start(bf16[96,8,1280]{2,1,0:T(8,128)(2,1)} %copy.67), calls=%async_computation.6 | async-start | bytes 3932160 | tf_op jit(solution)/shard_map/all_to_all | solution.py:67
  444.2 77.4 %all-reduce.6.cloned.1.call-start = ((), (), s32[]{:S(2)}) async-start(), calls=%async_computation.8 | async-start | bytes 2359296 | tf_op jit(solution)/shard_map/psum | solution.py:101
  476.9 6.2 copy-start.15
  476.9 6.1 copy-start.17
  476.9 6.1 copy-start.19
  521.6 5.3 copy-start.11
  521.6 5.3 copy-start.13
  521.6 5.3 copy-start.20
  530.5 35.3 %all-to-all-start.7 = ((bf16[96,8,1280]{2,1,0:T(8,128)(2,1)}), bf16[96,8,1280]{2,1,0:T(8,128)(2,1)}, u32[]{:S(2)}, u32[]{:S(2)}) async-start(bf16[96,8,1280]{2,1,0:T(8,128)(2,1)} %fusion.15), calls=%async_computation.7 | async-start | bytes 3932160 | tf_op jit(solution)/shard_map/all_to_all | solution.py:74
  537.3 6.8 %copy-start.5 = (bf16[96,8,1280]{2,1,0:T(8,128)(2,1)S(1)}, bf16[96,8,1280]{2,1,0:T(8,128)(2,1)}, u32[]{:S(2)}) copy-start(bf16[96,8,1280]{2,1,0:T(8,128)(2,1)} %copy-done.4) | copy-start | bytes 5898244
  537.3 6.8 %copy-start.14 = (bf16[768,768]{1,0:T(8,128)(2,1)S(1)}, bf16[768,768]{1,0:T(8,128)(2,1)}, u32[]{:S(2)}) copy-start(bf16[768,768]{1,0:T(8,128)(2,1)} %get-tuple-element.14) | copy-start | bytes 3538948
  537.3 6.8 %copy-start.21 = (bf16[768,768]{1,0:T(8,128)(2,1)S(1)}, bf16[768,768]{1,0:T(8,128)(2,1)}, u32[]{:S(2)}) copy-start(bf16[768,768]{1,0:T(8,128)(2,1)} %all-reduce.6.cloned.1.call-done) | copy-start | bytes 3538948
  537.3 6.8 %copy-start.22 = (f32[1280,768]{1,0:T(8,128)S(1)}, f32[1280,768]{1,0:T(8,128)}, u32[]{:S(2)}) copy-start(f32[1280,768]{1,0:T(8,128)} %fusion.62) | copy-start | bytes 11796484
  544.1 3.2 copy-start.12
  544.1 3.2 copy-start.23
  (3 other events, 7.7 us)
Sparse Core Ops, SparseCore 0:
  53.3 61.8 all-reduce.9
  239.0 79.3 all-reduce.7
  477.0 44.5 all-reduce.5
